TPU v7x, 32 devices: a whole 2x2x4 slice. The times are simulated.
32 devices in a mesh: gx: 8 (over z, x), gy: 4 (over y, core).
Axes of the slice: x: 2, y: 2, z: 4, core: 2. Of those that a mesh axis runs over, the one named last changes fastest.
Arguments:
- profiles: float32 [2, 32768, 128], P(None, ('gx', 'gy')), may hold values from 0.5 to 2
- radial: float32 [2, 128, 128], replicated, may hold values from -1 to 2
- rate_const: float32 [32768], P(('gx', 'gy')), may hold values from 0.02 to 0.2
- transfer_coef: float32 [32768], P(('gx', 'gy')), may hold values from 0.1 to 0.5
- live_count: int32 [32], P(('gx', 'gy')), may hold values from 256 to 1024, as said below
- send_lists: int32 [256, 128], P(('gx', 'gy')), may hold values from 0 to 1023, as said below
- cell_index: int32 [32768], P(('gx', 'gy')), may hold values from 0 to 131071
- contact_cols: int32 [256, 4], P(('gx', 'gy')), may hold values from 0 to 15, as said below
- contact_blocks: float32 [256, 4, 128, 128], P(('gx', 'gy')), may hold values from 0 to 0.006
- populations: float32 [7, 256, 128, 128], P(None, 'gx', 'gy'), may hold values from -1.8 to 1.8
Outputs:
- profiles_out: float32 [2, 32768, 128], P(None, ('gx', 'gy'))
- populations_out: float32 [7, 256, 128, 128], P(None, 'gx', 'gy')
Inputs may be any that keep to these rules, and one draw needn't show every extreme that they name: `live_count`: each tile's count is a multiple of 128, at least a quarter of its slots, and some tile is full. `send_lists`: every entry names a live slot of the sending tile. `contact_cols`: blocks 0 to 7 are the tile's own, block 8 + n is ghost block n; every ghost block is named by some row block.
All inputs are finite; a program needn't handle non-finite values.
Results may differ from a plain program's by a relative error of at most 0.0001.
Values sent between devices are 32-bit elements; how exact they have to be, the bound alone decides.
A program may use at most 128 MiB of HBM per device.

v0:
```python
import jax
import jax.numpy as jnp
import numpy as np
from jax import lax
from jax.experimental import pallas as pl
from jax.experimental.pallas import tpu as pltpu
from jax.sharding import PartitionSpec as P

BLK = 128
SHELL = 16
STEPS = 3
OFFSETS = ((-1, -1), (-1, 0), (-1, 1), (0, -1), (0, 1), (1, -1), (1, 0), (1, 1))
SIDES = ((1, 0), (-1, 0), (0, 1), (0, -1))
MESH = pl.DeviceIdType.MESH
F32 = jnp.float32
BF16 = jnp.bfloat16


def high_part(value):
    return value.astype(BF16).astype(F32)


def dot(a, b):
    return jnp.dot(a, b, preferred_element_type=F32)


def roll(value, amount, axis):
    amount = amount % value.shape[axis]
    return value if amount == 0 else pltpu.roll(value, amount, axis)


def kernel(
    live_ref, cols_ref, rate_ref, coef_ref, cell_ref, lists_ref, radial_ref,
    prof_in, blocks_in, pop_in,
    prof_out, pop_out,
    prof, pop, raw, blocks, mixer, pick, pick_t, listed, zmask, coef, rate_c,
    shells, ext, theta, theta_s, cell_ex, ex_s, q_ref,
    send_g, recv_g, send_h, recv_h,
    in_sems, out_sems, gs_sems, gr_sems, hs_sems, hr_sems,
):
    own = prof.shape[1] // BLK
    cx, cy, nz = theta.shape
    rows = cx * cy
    kb = cols_ref.shape[1]
    ix, iy = lax.axis_index("gx"), lax.axis_index("gy")
    sx, sy = lax.axis_size("gx"), lax.axis_size("gy")

    def there(ox, oy):
        x, y = ix + ox, iy + oy
        return (x >= 0) & (x < sx) & (y >= 0) & (y < sy)

    load_prof = pltpu.make_async_copy(prof_in, prof, in_sems.at[0])
    load_pop = pltpu.make_async_copy(pop_in, pop.at[0, :, pl.ds(1, cx)], in_sems.at[1])
    load_blocks = pltpu.make_async_copy(blocks_in, raw, in_sems.at[2])
    load_prof.start()
    load_pop.start()
    load_blocks.start()

    recv_g[...] = jnp.zeros_like(recv_g)
    recv_h[...] = jnp.zeros_like(recv_h)
    barrier = pltpu.get_barrier_semaphore()
    for ox, oy in OFFSETS:
        @pl.when(there(ox, oy))
        def _():
            pl.semaphore_signal(barrier, inc=1, device_id=(ix + ox, iy + oy), device_id_type=MESH)

    live_count = live_ref[0]
    sub = lax.broadcasted_iota(jnp.int32, (BLK, BLK), 0)
    lane = lax.broadcasted_iota(jnp.int32, (BLK, BLK), 1)
    lane_f = lane.astype(F32)
    sub_f = sub.astype(F32)
    in_shell = lane >= BLK - SHELL
    in_live = (lane >= BLK - 3 * SHELL) & (lane < BLK - 2 * SHELL)

    def one_hot(match):
        return jnp.where(match, 1.0, 0.0).astype(BF16)

    def column(row):
        return jnp.broadcast_to(row, (BLK, BLK)).T

    def setup(c, carry):
        span = pl.ds(pl.multiple_of(c * BLK, BLK), BLK)
        at = pl.ds(c, 1)
        cell = cell_ref[at, :]
        row_col = column((cell // nz).astype(F32))
        z_col = column((cell % nz).astype(F32))
        list_col = column(lists_ref[at, :].astype(F32))
        zmask[span, :] = jnp.where(z_col == lane_f, 1.0, 0.0)
        coef[span, :] = jnp.where(sub + c * BLK < live_count, column(coef_ref[at, :]), 0.0)
        rate_c[span, :] = column(rate_ref[at, :])
        for d in range(rows // BLK):
            pick[span, d * BLK:(d + 1) * BLK] = one_hot(row_col == lane_f + d * BLK)
        for d in range(own):
            listed[span, d * BLK:(d + 1) * BLK] = one_hot(list_col == lane_f + d * BLK)
        return carry

    lax.fori_loop(0, own, setup, 0)

    def setup_t(c, carry):
        span = pl.ds(pl.multiple_of(c * BLK, BLK), BLK)
        base = sub_f + (c * BLK).astype(F32)
        for d in range(own):
            row = (cell_ref[d:d + 1, :] // nz).astype(F32)
            pick_t[span, d * BLK:(d + 1) * BLK] = one_hot(jnp.broadcast_to(row, (BLK, BLK)) == base)
        return carry

    lax.fori_loop(0, rows // BLK, setup_t, 0)

    for c in range(2):
        value = radial_ref[c]
        high = value.astype(BF16)
        low = (value - high.astype(F32)).astype(BF16)
        mixer[c, :BLK, :BLK] = high
        mixer[c, :BLK, BLK:] = low
        mixer[c, BLK:, :BLK] = high
        mixer[c, BLK:, BLK:] = jnp.zeros_like(high)

    load_blocks.wait()

    def split_block(i, carry):
        value = raw[i]
        high = value.astype(BF16)
        blocks[i, :, :BLK] = high
        blocks[i, :, BLK:] = (value - high.astype(F32)).astype(BF16)
        return carry

    lax.fori_loop(0, own * kb, split_block, 0)
    load_prof.wait()
    load_pop.wait()
    count_x = 1 + (ix > 0).astype(jnp.int32) + (ix < sx - 1).astype(jnp.int32)
    count_y = 1 + (iy > 0).astype(jnp.int32) + (iy < sy - 1).astype(jnp.int32)
    pl.semaphore_wait(barrier, count_x * count_y - 1)

    def ghost_copy(step, n):
        ox, oy = OFFSETS[n]
        return pltpu.make_async_remote_copy(
            src_ref=send_g.at[step, n], dst_ref=recv_g.at[step, n],
            send_sem=gs_sems.at[step, n], recv_sem=gr_sems.at[step, n],
            device_id=(ix + ox, iy + oy), device_id_type=MESH)

    def halo_copy(step, n):
        ox, oy = SIDES[n]
        return pltpu.make_async_remote_copy(
            src_ref=send_h.at[step, n], dst_ref=recv_h.at[step, n],
            send_sem=hs_sems.at[step, n], recv_sem=hr_sems.at[step, n],
            device_id=(ix + ox, iy + oy), device_id_type=MESH)

    def one_step(step, carry):
        cur = lax.rem(step, 2)
        nxt = 1 - cur

        def prepare(r, carry):
            span = pl.ds(pl.multiple_of(r * BLK, BLK), BLK)
            value = jnp.where(in_shell, prof[0, span, :], 0.0)
            high = high_part(value)
            low = value - high
            mid = high_part(low)
            low_rolled = roll(low, -SHELL, 1)
            shells[span, :] = (high + roll(mid, -SHELL, 1) + roll(low - mid, -2 * SHELL, 1)).astype(BF16)
            live = sub + r * BLK < live_count
            marked = high + jnp.where(in_live, 1.0, 0.0)
            ext[r, :BLK, :] = jnp.where(live, marked + low_rolled, 0.0).astype(BF16)
            ext[r, BLK:, :] = jnp.where(live, marked, 0.0).astype(BF16)
            return carry

        lax.fori_loop(0, own, prepare, 0)

        def gather_ghosts(n, carry):
            span = pl.ds(pl.multiple_of(n * BLK, BLK), BLK)
            found = dot(listed[span, :], shells[...])
            found = found + roll(found, SHELL, 1) + roll(found, 2 * SHELL, 1)
            found = jnp.where(in_shell, found, 0.0)
            packed = jnp.zeros((SHELL, BLK), F32)
            for j in range(BLK // SHELL):
                packed = packed + roll(found[j * SHELL:(j + 1) * SHELL, :], (j + 1) * SHELL, 1)
            send_g[step, n] = packed
            return carry

        lax.fori_loop(0, 8, gather_ghosts, 0)
        for n in range(8):
            @pl.when(there(*OFFSETS[n]))
            def _():
                ghost_copy(step, n).start()

        def sum_theta(x, carry):
            total = pop[cur, 0, x + 1]
            for i in range(1, 7):
                total = total + pop[cur, i, x + 1]
            theta[x] = total
            span = pl.ds(pl.multiple_of(x * cy, cy), cy)
            high = total.astype(BF16)
            theta_s[span, :nz] = high
            theta_s[span, nz:] = (total - high.astype(F32)).astype(BF16)
            return carry

        lax.fori_loop(0, cx, sum_theta, 0)
        ones = jnp.ones((2 * nz, BLK), BF16)

        def gather_theta(c, carry):
            span = pl.ds(pl.multiple_of(c * 2 * BLK, 2 * BLK), 2 * BLK)
            found = dot(pick[span, :], theta_s[...])
            mask = zmask[span, :]
            kept = jnp.concatenate([found[:, :nz] * mask, found[:, nz:] * mask], axis=1).astype(BF16)
            at_cell = dot(kept, ones)
            last = jnp.broadcast_to(prof[0, span, BLK - 1:], (2 * BLK, BLK))
            value = coef[span, :] * (at_cell - last)
            cell_ex[span, :] = value
            value = value * mask
            high = value.astype(BF16)
            ex_s[span, :nz] = high
            ex_s[span, nz:] = (value - high.astype(F32)).astype(BF16)
            return carry

        lax.fori_loop(0, own // 2, gather_theta, 0)
        slabs = 2 * BLK // cy

        def scatter(c, carry):
            span = pl.ds(pl.multiple_of(c * 2 * BLK, 2 * BLK), 2 * BLK)
            found = dot(pick_t[span, :], ex_s[...])
            some = pl.ds(c * slabs, slabs)
            total = (found[:, :nz] + found[:, nz:]).reshape(slabs, cy, nz)
            q_ref[some] = 1.25 * theta[some] - 0.5 * total
            return carry

        lax.fori_loop(0, rows // (2 * BLK), scatter, 0)
        zlane = lax.broadcasted_iota(jnp.int32, (cy, nz), 1)

        def stream(x, carry):
            q = q_ref[x]
            part = 0.125 * q
            pop[nxt, 0, x + 1] = 0.25 * (q - pop[cur, 0, x + 1])
            pop[nxt, 1, x + 2] = part - 0.25 * pop[cur, 1, x + 1]
            pop[nxt, 2, x] = part - 0.25 * pop[cur, 2, x + 1]
            up = roll(part - 0.25 * pop[cur, 3, x + 1], 1, 0)
            down = roll(part - 0.25 * pop[cur, 4, x + 1], -1, 0)
            pop[nxt, 3, x + 1] = up
            pop[nxt, 4, x + 1] = down
            send_h[step, 2, pl.ds(x, 1), :] = up[:1]
            send_h[step, 3, pl.ds(x, 1), :] = down[cy - 1:]
            above = roll(part - 0.25 * pop[cur, 5, x + 1], 1, 1)
            below = roll(part - 0.25 * pop[cur, 6, x + 1], -1, 1)
            pop[nxt, 5, x + 1] = jnp.where(zlane == 0, 0.0, above)
            pop[nxt, 6, x + 1] = jnp.where(zlane == nz - 1, 0.0, below)
            return carry

        lax.fori_loop(0, cx, stream, 0)
        send_h[step, 0] = pop[nxt, 1, cx + 1]
        send_h[step, 1] = pop[nxt, 2, 0]
        for n in range(4):
            @pl.when(there(*SIDES[n]))
            def _():
                halo_copy(step, n).start()

        for n in range(8):
            ox, oy = OFFSETS[n]
            here = there(-ox, -oy)

            @pl.when(here)
            def _():
                ghost_copy(step, n).wait_recv()

        shell16 = lax.broadcasted_iota(jnp.int32, (SHELL, BLK), 1)
        ghost_shell = shell16 >= BLK - SHELL
        ghost_live = (shell16 >= BLK - 3 * SHELL) & (shell16 < BLK - 2 * SHELL)
        for n in range(8):
            ox, oy = OFFSETS[n]
            mark = jnp.where(ghost_live, there(-ox, -oy).astype(F32), 0.0)
            packed = recv_g[step, n]
            for j in range(BLK // SHELL):
                value = jnp.where(ghost_shell, roll(packed, BLK - (j + 1) * SHELL, 1), 0.0)
                high = high_part(value)
                marked = high + mark
                ext[own + n, j * SHELL:(j + 1) * SHELL, :] = (marked + roll(value - high, -SHELL, 1)).astype(BF16)
                ext[own + n, BLK + j * SHELL:BLK + (j + 1) * SHELL, :] = marked.astype(BF16)

        def update(r, carry):
            span = pl.ds(pl.multiple_of(r * BLK, BLK), BLK)
            temp = prof[0, span, :]
            conc = prof[1, span, :]
            mixed = []
            for c, value in enumerate((temp, conc)):
                high = value.astype(BF16)
                low = (value - high.astype(F32)).astype(BF16)
                both = dot(jnp.concatenate([high, low], axis=1), mixer[c])
                mixed.append(both[:, :BLK] + both[:, BLK:])
            total = jnp.zeros((BLK, BLK), F32)
            for k in range(kb):
                total = total + dot(blocks[r * kb + k], ext[cols_ref[r, k]])
            contact = total + roll(total, SHELL, 1) - roll(total, 2 * SHELL, 1) * temp
            rate = rate_c[span, :] * conc * jnp.exp(0.5 * jnp.tanh(temp - 1.0))
            new_temp = mixed[0] + rate + jnp.where(in_shell, contact, 0.0)
            new_temp = new_temp + jnp.where(lane == BLK - 1, cell_ex[span, :], 0.0)
            live = sub + r * BLK < live_count
            prof[0, span, :] = jnp.where(live, new_temp, temp)
            prof[1, span, :] = jnp.where(live, mixed[1] - rate, conc)
            return carry

        lax.fori_loop(0, own, update, 0)

        for n in range(4):
            ox, oy = SIDES[n]

            @pl.when(there(-ox, -oy))
            def _():
                halo_copy(step, n).wait_recv()

        pop[nxt, 1, 1] = recv_h[step, 0]
        pop[nxt, 2, cx] = recv_h[step, 1]

        def edges(x, carry):
            pop[nxt, 3, x + 1, pl.ds(0, 1), :] = recv_h[step, 2, pl.ds(x, 1), :]
            pop[nxt, 4, x + 1, pl.ds(cy - 1, 1), :] = recv_h[step, 3, pl.ds(x, 1), :]
            return carry

        lax.fori_loop(0, cx, edges, 0)
        return carry

    lax.fori_loop(0, STEPS, one_step, 0)
    store_prof = pltpu.make_async_copy(prof, prof_out, out_sems.at[0])
    store_pop = pltpu.make_async_copy(pop.at[STEPS % 2, :, pl.ds(1, cx)], pop_out, out_sems.at[1])
    store_prof.start()
    store_pop.start()
    for step in range(STEPS):
        for n in range(8):
            @pl.when(there(*OFFSETS[n]))
            def _():
                ghost_copy(step, n).wait_send()
        for n in range(4):
            @pl.when(there(*SIDES[n]))
            def _():
                halo_copy(step, n).wait_send()
    store_prof.wait()
    store_pop.wait()


def on_device(
    profiles, radial, rate_const, transfer_coef, live_count, send_lists, cell_index, contact_cols,
    contact_blocks, populations,
):
    slots = profiles.shape[1]
    own = slots // BLK
    kb = contact_cols.shape[1]
    _, cx, cy, nz = populations.shape
    rows = cx * cy
    vmem = pl.BlockSpec(memory_space=pltpu.VMEM)
    smem = pl.BlockSpec(memory_space=pltpu.SMEM)
    anywhere = pl.BlockSpec(memory_space=pl.ANY)
    return pl.pallas_call(
        kernel,
        out_shape=(
            jax.ShapeDtypeStruct(profiles.shape, F32),
            jax.ShapeDtypeStruct(populations.shape, F32),
        ),
        in_specs=[smem, smem, vmem, vmem, vmem, vmem, vmem, anywhere, anywhere, anywhere],
        out_specs=(anywhere, anywhere),
        scratch_shapes=[
            pltpu.VMEM(profiles.shape, F32),
            pltpu.VMEM((2, 7, cx + 2, cy, nz), F32),
            pltpu.VMEM((own * kb, BLK, BLK), F32),
            pltpu.VMEM((own * kb, BLK, 2 * BLK), BF16),
            pltpu.VMEM((2, 2 * BLK, 2 * BLK), BF16),
            pltpu.VMEM((slots, rows), BF16),
            pltpu.VMEM((rows, slots), BF16),
            pltpu.VMEM((8 * BLK, slots), BF16),
            pltpu.VMEM((slots, nz), F32),
            pltpu.VMEM((slots, BLK), F32),
            pltpu.VMEM((slots, BLK), F32),
            pltpu.VMEM((slots, BLK), BF16),
            pltpu.VMEM((own + 8, 2 * BLK, BLK), BF16),
            pltpu.VMEM((cx, cy, nz), F32),
            pltpu.VMEM((rows, 2 * nz), BF16),
            pltpu.VMEM((slots, BLK), F32),
            pltpu.VMEM((slots, 2 * nz), BF16),
            pltpu.VMEM((cx, cy, nz), F32),
            pltpu.VMEM((STEPS, 8, SHELL, BLK), F32),
            pltpu.VMEM((STEPS, 8, SHELL, BLK), F32),
            pltpu.VMEM((STEPS, 4, cx, nz), F32),
            pltpu.VMEM((STEPS, 4, cx, nz), F32),
            pltpu.SemaphoreType.DMA((3,)),
            pltpu.SemaphoreType.DMA((2,)),
            pltpu.SemaphoreType.DMA((STEPS, 8)),
            pltpu.SemaphoreType.DMA((STEPS, 8)),
            pltpu.SemaphoreType.DMA((STEPS, 4)),
            pltpu.SemaphoreType.DMA((STEPS, 4)),
        ],
        compiler_params=pltpu.CompilerParams(
            collective_id=0, has_side_effects=True, vmem_limit_bytes=48 * 1024 * 1024
        ),
    )(
        live_count,
        contact_cols,
        rate_const.reshape(own, BLK),
        transfer_coef.reshape(own, BLK),
        cell_index.reshape(own, BLK),
        send_lists,
        radial,
        profiles,
        contact_blocks.reshape(own * kb, BLK, BLK),
        populations,
    )


def solution(mesh):
    return jax.shard_map(
        on_device,
        mesh=mesh,
        in_specs=(
            P(None, ("gx", "gy"), None),
            P(),
            P(("gx", "gy")),
            P(("gx", "gy")),
            P(("gx", "gy")),
            P(("gx", "gy"), None),
            P(("gx", "gy")),
            P(("gx", "gy"), None),
            P(("gx", "gy"), None, None, None),
            P(None, "gx", "gy", None),
        ),
        out_specs=(P(None, ("gx", "gy"), None), P(None, "gx", "gy", None)),
        check_vma=False,
    )
```

profile of v0, /device:TPU:1, one launch (start us, length us, event | category | flops | bytes accessed | tf_op | source)
XLA Modules:
  0.0 68.1 jit_solution(11178248313910413768)
XLA Ops:
  1.3 0.8 %copy.12.cols_ref = s32[8,4]{1,0:T(8,128)S(1)} copy(s32[8,4]{0,1:T(4,128)} %param.17) | data formatting | bytes 256 | tf_op args[7]
  2.0 0.0 copy-start
  2.0 1.6 %copy-done = f32[8,4,128,128]{3,2,1,0:T(8,128)S(1)} copy-done((f32[8,4,128,128]{3,2,1,0:T(8,128)S(1)}, f32[8,4,128,128]{3,2,1,0:T(8,128)}, u32[]{:S(2)}) %copy-start) | copy-done | bytes 2097176
  3.6 0.0 copy-start.1
  3.6 1.2 %copy-done.1 = f32[2,1024,128]{2,1,0:T(8,128)S(1)} copy-done((f32[2,1024,128]{2,1,0:T(8,128)S(1)}, f32[2,1024,128]{2,1,0:T(8,128)}, u32[]{:S(2)}) %copy-start.1) | copy-done | bytes 1048600
  4.8 0.0 copy-start.2
  4.9 0.9 %copy-done.2 = f32[2,128,128]{2,1,0:T(8,128)S(1)} copy-done((f32[2,128,128]{2,1,0:T(8,128)S(1)}, f32[2,128,128]{2,1,0:T(8,128)}, u32[]{:S(2)}) %copy-start.2) | copy-done | bytes 131096
  5.8 0.0 copy-start.3
  5.8 0.7 %copy-done.3 = f32[1024]{0:T(1024)S(1)} copy-done((f32[1024]{0:T(1024)S(1)}, f32[1024]{0:T(1024)}, u32[]{:S(2)}) %copy-start.3) | copy-done | bytes 4120
  6.4 0.0 copy-start.4
  6.4 0.7 %copy-done.4 = f32[1024]{0:T(1024)S(1)} copy-done((f32[1024]{0:T(1024)S(1)}, f32[1024]{0:T(1024)}, u32[]{:S(2)}) %copy-start.4) | copy-done | bytes 4120
  7.1 0.0 copy-start.5
  7.1 0.7 %copy-done.5 = s32[1024]{0:T(1024)S(1)} copy-done((s32[1024]{0:T(1024)S(1)}, s32[1024]{0:T(1024)}, u32[]{:S(2)}) %copy-start.5) | copy-done | bytes 4120
  7.8 0.0 copy-start.6
  7.8 0.7 %copy-done.6 = s32[8,128]{1,0:T(8,128)S(1)} copy-done((s32[8,128]{1,0:T(8,128)S(1)}, s32[8,128]{1,0:T(8,128)}, u32[]{:S(2)}) %copy-start.6) | copy-done | bytes 4120
  8.5 54.2 %shard_map.113 = (f32[2,1024,128]{2,1,0:T(8,128)S(1)}, f32[7,32,32,128]{3,2,1,0:T(8,128)}) custom-call(s32[1]{0:T(128)S(6)} %copy.15.live_ref, s32[8,4]{1,0:T(8,128)S(1)} %copy.12.cols_ref, f32[8,128]{1,0:T(8,128)S(1)} %bitcast.5, f32[8,128]{1,0:T(8,128)S(1)} %bitcast.6, s32[8,128]{1,0:T(8,128)S(1)} %bitcast.7, s32[8,128]{1,0:T(8,128)S(1)} %copy-done.6, ...), custom_call_target="tpu_custom_call" | custom-call | tf_op jit(solution)/shard_map/pallas_call | solution.py:348
  62.7 1.0 %copy.16 = f32[2,1024,128]{2,1,0:T(8,128)} copy(f32[2,1024,128]{2,1,0:T(8,128)S(1)} %get-tuple-element.4) | data formatting | bytes 2097152
  63.7 4.4 %copy.17 = f32[7,32,32,128]{3,2,1,0:T(8,128)} copy(f32[7,32,32,128]{3,2,1,0:T(8,128)} %get-tuple-element.5) | data formatting | bytes 7340032
Async XLA Ops:
  2.0 1.6 %copy-start = (f32[8,4,128,128]{3,2,1,0:T(8,128)S(1)}, f32[8,4,128,128]{3,2,1,0:T(8,128)}, u32[]{:S(2)}) copy-start(f32[8,4,128,128]{3,2,1,0:T(8,128)} %param.18) | copy-start | bytes 6291460
  3.6 1.2 %copy-start.1 = (f32[2,1024,128]{2,1,0:T(8,128)S(1)}, f32[2,1024,128]{2,1,0:T(8,128)}, u32[]{:S(2)}) copy-start(f32[2,1024,128]{2,1,0:T(8,128)} %prof_in.1) | copy-start | bytes 3145732
  4.8 0.9 %copy-start.2 = (f32[2,128,128]{2,1,0:T(8,128)S(1)}, f32[2,128,128]{2,1,0:T(8,128)}, u32[]{:S(2)}) copy-start(f32[2,128,128]{2,1,0:T(8,128)} %radial_ref.1) | copy-start | bytes 393220
  5.8 0.7 %copy-start.3 = (f32[1024]{0:T(1024)S(1)}, f32[1024]{0:T(1024)}, u32[]{:S(2)}) copy-start(f32[1024]{0:T(1024)} %param.12) | copy-start | bytes 12292
  6.4 0.7 %copy-start.4 = (f32[1024]{0:T(1024)S(1)}, f32[1024]{0:T(1024)}, u32[]{:S(2)}) copy-start(f32[1024]{0:T(1024)} %param.13) | copy-start | bytes 12292
  7.1 0.7 %copy-start.5 = (s32[1024]{0:T(1024)S(1)}, s32[1024]{0:T(1024)}, u32[]{:S(2)}) copy-start(s32[1024]{0:T(1024)} %param.16) | copy-start | bytes 12292
  7.8 0.7 %copy-start.6 = (s32[8,128]{1,0:T(8,128)S(1)}, s32[8,128]{1,0:T(8,128)}, u32[]{:S(2)}) copy-start(s32[8,128]{1,0:T(8,128)} %lists_ref.1) | copy-start | bytes 12292
where the time goes:
time: 68.5 us; the launch traced here: 68.1 us
  Pallas kernels  54.2 us (79%)
  local copies, waits for them, and re-layouts  12.6 us (18%)
  between operations  1.29 us (2%)
    pallas_call x1, Pallas kernels, on_device(): pl.pallas_call(kernel, out_shape=(jax.ShapeDtypeStruct(profiles.shape, F3...  54.2 us
    unnamed x17, local copies, waits for them, and re-layouts  12.6 us

commit v1 on v0

--- a/solution.py
+++ b/solution.py
@@ -30,18 +30,19 @@
 
 
 def kernel(
-    live_ref, cols_ref, rate_ref, coef_ref, cell_ref, lists_ref, radial_ref,
+    live_ref, cols_ref, rate_in, coef_in, cell_in, lists_in, radial_in,
     prof_in, blocks_in, pop_in,
-    prof_out, pop_out,
-    prof, pop, raw, blocks, mixer, pick, pick_t, listed, zmask, coef, rate_c,
+    prof, pop_b,
+    pop_a, rate_ref, coef_ref, cell_ref, lists_ref, radial_ref,
+    raw, blocks, mixer, pick, pick_t, listed, zmask, coef, rate_c,
     shells, ext, theta, theta_s, cell_ex, ex_s, q_ref,
     send_g, recv_g, send_h, recv_h,
-    in_sems, out_sems, gs_sems, gr_sems, hs_sems, hr_sems,
+    in_sems, gs_sems, gr_sems, hs_sems, hr_sems,
 ):
     own = prof.shape[1] // BLK
     cx, cy, nz = theta.shape
     rows = cx * cy
-    kb = cols_ref.shape[1]
+    kb = cols_ref.shape[0]
     ix, iy = lax.axis_index("gx"), lax.axis_index("gy")
     sx, sy = lax.axis_size("gx"), lax.axis_size("gy")
 
@@ -49,9 +50,17 @@
         x, y = ix + ox, iy + oy
         return (x >= 0) & (x < sx) & (y >= 0) & (y < sy)
 
+    small = [
+        pltpu.make_async_copy(source, target, in_sems.at[3 + i])
+        for i, (source, target) in enumerate((
+            (lists_in, lists_ref), (cell_in, cell_ref), (coef_in, coef_ref), (rate_in, rate_ref),
+            (radial_in, radial_ref)))
+    ]
     load_prof = pltpu.make_async_copy(prof_in, prof, in_sems.at[0])
-    load_pop = pltpu.make_async_copy(pop_in, pop.at[0, :, pl.ds(1, cx)], in_sems.at[1])
+    load_pop = pltpu.make_async_copy(pop_in, pop_a.at[:, pl.ds(1, cx)], in_sems.at[1])
     load_blocks = pltpu.make_async_copy(blocks_in, raw, in_sems.at[2])
+    for load in small:
+        load.start()
     load_prof.start()
     load_pop.start()
     load_blocks.start()
@@ -69,6 +78,8 @@
     lane = lax.broadcasted_iota(jnp.int32, (BLK, BLK), 1)
     lane_f = lane.astype(F32)
     sub_f = sub.astype(F32)
+    wide_sub = lax.broadcasted_iota(jnp.int32, (2 * BLK, BLK), 0)
+    wide_lane = lax.broadcasted_iota(jnp.int32, (2 * BLK, BLK), 1)
     in_shell = lane >= BLK - SHELL
     in_live = (lane >= BLK - 3 * SHELL) & (lane < BLK - 2 * SHELL)
 
@@ -77,6 +88,9 @@
 
     def column(row):
         return jnp.broadcast_to(row, (BLK, BLK)).T
+
+    for load in small:
+        load.wait()
 
     def setup(c, carry):
         span = pl.ds(pl.multiple_of(c * BLK, BLK), BLK)
@@ -115,18 +129,7 @@
         mixer[c, BLK:, :BLK] = high
         mixer[c, BLK:, BLK:] = jnp.zeros_like(high)
 
-    load_blocks.wait()
-
-    def split_block(i, carry):
-        value = raw[i]
-        high = value.astype(BF16)
-        blocks[i, :, :BLK] = high
-        blocks[i, :, BLK:] = (value - high.astype(F32)).astype(BF16)
-        return carry
-
-    lax.fori_loop(0, own * kb, split_block, 0)
     load_prof.wait()
-    load_pop.wait()
     count_x = 1 + (ix > 0).astype(jnp.int32) + (ix < sx - 1).astype(jnp.int32)
     count_y = 1 + (iy > 0).astype(jnp.int32) + (iy < sy - 1).astype(jnp.int32)
     pl.semaphore_wait(barrier, count_x * count_y - 1)
@@ -145,10 +148,7 @@
             send_sem=hs_sems.at[step, n], recv_sem=hr_sems.at[step, n],
             device_id=(ix + ox, iy + oy), device_id_type=MESH)
 
-    def one_step(step, carry):
-        cur = lax.rem(step, 2)
-        nxt = 1 - cur
-
+    def one_step(step, old, new):
         def prepare(r, carry):
             span = pl.ds(pl.multiple_of(r * BLK, BLK), BLK)
             value = jnp.where(in_shell, prof[0, span, :], 0.0)
@@ -166,43 +166,50 @@
         lax.fori_loop(0, own, prepare, 0)
 
         def gather_ghosts(n, carry):
-            span = pl.ds(pl.multiple_of(n * BLK, BLK), BLK)
-            found = dot(listed[span, :], shells[...])
-            found = found + roll(found, SHELL, 1) + roll(found, 2 * SHELL, 1)
-            found = jnp.where(in_shell, found, 0.0)
-            packed = jnp.zeros((SHELL, BLK), F32)
-            for j in range(BLK // SHELL):
-                packed = packed + roll(found[j * SHELL:(j + 1) * SHELL, :], (j + 1) * SHELL, 1)
-            send_g[step, n] = packed
-            return carry
-
-        lax.fori_loop(0, 8, gather_ghosts, 0)
+            span = pl.ds(pl.multiple_of(n * 4 * BLK, 4 * BLK), 4 * BLK)
+            several = dot(listed[span, :], shells[...])
+            for m in range(4):
+                found = several[m * BLK:(m + 1) * BLK, :]
+                found = found + roll(found, SHELL, 1) + roll(found, 2 * SHELL, 1)
+                found = jnp.where(in_shell, found, 0.0)
+                packed = jnp.zeros((SHELL, BLK), F32)
+                for j in range(BLK // SHELL):
+                    packed = packed + roll(found[j * SHELL:(j + 1) * SHELL, :], (j + 1) * SHELL, 1)
+                send_g[step, n * 4 + m] = packed
+            return carry
+
+        lax.fori_loop(0, 2, gather_ghosts, 0)
         for n in range(8):
             @pl.when(there(*OFFSETS[n]))
             def _():
                 ghost_copy(step, n).start()
 
-        def sum_theta(x, carry):
-            total = pop[cur, 0, x + 1]
-            for i in range(1, 7):
-                total = total + pop[cur, i, x + 1]
-            theta[x] = total
-            span = pl.ds(pl.multiple_of(x * cy, cy), cy)
-            high = total.astype(BF16)
-            theta_s[span, :nz] = high
-            theta_s[span, nz:] = (total - high.astype(F32)).astype(BF16)
-            return carry
-
-        lax.fori_loop(0, cx, sum_theta, 0)
+        if step == 0:
+            load_pop.wait()
+
+        def sum_theta(c, carry):
+            for u in range(4):
+                x = c * 4 + u
+                total = old[0, x + 1]
+                for i in range(1, 7):
+                    total = total + old[i, x + 1]
+                theta[x] = total
+                span = pl.ds(pl.multiple_of(x * cy, cy), cy)
+                high = total.astype(BF16)
+                theta_s[span, :nz] = high
+                theta_s[span, nz:] = (total - high.astype(F32)).astype(BF16)
+            return carry
+
+        lax.fori_loop(0, cx // 4, sum_theta, 0)
         ones = jnp.ones((2 * nz, BLK), BF16)
 
         def gather_theta(c, carry):
-            span = pl.ds(pl.multiple_of(c * 2 * BLK, 2 * BLK), 2 * BLK)
+            span = pl.ds(pl.multiple_of(c * 4 * BLK, 4 * BLK), 4 * BLK)
             found = dot(pick[span, :], theta_s[...])
             mask = zmask[span, :]
             kept = jnp.concatenate([found[:, :nz] * mask, found[:, nz:] * mask], axis=1).astype(BF16)
             at_cell = dot(kept, ones)
-            last = jnp.broadcast_to(prof[0, span, BLK - 1:], (2 * BLK, BLK))
+            last = jnp.broadcast_to(prof[0, span, BLK - 1:], (4 * BLK, BLK))
             value = coef[span, :] * (at_cell - last)
             cell_ex[span, :] = value
             value = value * mask
@@ -211,45 +218,59 @@
             ex_s[span, nz:] = (value - high.astype(F32)).astype(BF16)
             return carry
 
-        lax.fori_loop(0, own // 2, gather_theta, 0)
-        slabs = 2 * BLK // cy
+        lax.fori_loop(0, own // 4, gather_theta, 0)
+        slabs = 4 * BLK // cy
 
         def scatter(c, carry):
-            span = pl.ds(pl.multiple_of(c * 2 * BLK, 2 * BLK), 2 * BLK)
+            span = pl.ds(pl.multiple_of(c * 4 * BLK, 4 * BLK), 4 * BLK)
             found = dot(pick_t[span, :], ex_s[...])
             some = pl.ds(c * slabs, slabs)
             total = (found[:, :nz] + found[:, nz:]).reshape(slabs, cy, nz)
             q_ref[some] = 1.25 * theta[some] - 0.5 * total
             return carry
 
-        lax.fori_loop(0, rows // (2 * BLK), scatter, 0)
+        lax.fori_loop(0, rows // (4 * BLK), scatter, 0)
         zlane = lax.broadcasted_iota(jnp.int32, (cy, nz), 1)
 
-        def stream(x, carry):
-            q = q_ref[x]
-            part = 0.125 * q
-            pop[nxt, 0, x + 1] = 0.25 * (q - pop[cur, 0, x + 1])
-            pop[nxt, 1, x + 2] = part - 0.25 * pop[cur, 1, x + 1]
-            pop[nxt, 2, x] = part - 0.25 * pop[cur, 2, x + 1]
-            up = roll(part - 0.25 * pop[cur, 3, x + 1], 1, 0)
-            down = roll(part - 0.25 * pop[cur, 4, x + 1], -1, 0)
-            pop[nxt, 3, x + 1] = up
-            pop[nxt, 4, x + 1] = down
-            send_h[step, 2, pl.ds(x, 1), :] = up[:1]
-            send_h[step, 3, pl.ds(x, 1), :] = down[cy - 1:]
-            above = roll(part - 0.25 * pop[cur, 5, x + 1], 1, 1)
-            below = roll(part - 0.25 * pop[cur, 6, x + 1], -1, 1)
-            pop[nxt, 5, x + 1] = jnp.where(zlane == 0, 0.0, above)
-            pop[nxt, 6, x + 1] = jnp.where(zlane == nz - 1, 0.0, below)
-            return carry
-
-        lax.fori_loop(0, cx, stream, 0)
-        send_h[step, 0] = pop[nxt, 1, cx + 1]
-        send_h[step, 1] = pop[nxt, 2, 0]
+        def stream(c, carry):
+            for u in range(2):
+                x = c * 2 + u
+                q = q_ref[x]
+                part = 0.125 * q
+                new[0, x + 1] = 0.25 * (q - old[0, x + 1])
+                new[1, x + 2] = part - 0.25 * old[1, x + 1]
+                new[2, x] = part - 0.25 * old[2, x + 1]
+                up = roll(part - 0.25 * old[3, x + 1], 1, 0)
+                down = roll(part - 0.25 * old[4, x + 1], -1, 0)
+                new[3, x + 1] = up
+                new[4, x + 1] = down
+                send_h[step, 2, pl.ds(x, 1), :] = up[:1]
+                send_h[step, 3, pl.ds(x, 1), :] = down[cy - 1:]
+                above = roll(part - 0.25 * old[5, x + 1], 1, 1)
+                below = roll(part - 0.25 * old[6, x + 1], -1, 1)
+                new[5, x + 1] = jnp.where(zlane == 0, 0.0, above)
+                new[6, x + 1] = jnp.where(zlane == nz - 1, 0.0, below)
+            return carry
+
+        lax.fori_loop(0, cx // 2, stream, 0)
+        send_h[step, 0] = new[1, cx + 1]
+        send_h[step, 1] = new[2, 0]
         for n in range(4):
             @pl.when(there(*SIDES[n]))
             def _():
                 halo_copy(step, n).start()
+
+        if step == 0:
+            load_blocks.wait()
+
+            def split_block(i, carry):
+                value = raw[i]
+                high = value.astype(BF16)
+                blocks[i, :, :BLK] = high
+                blocks[i, :, BLK:] = (value - high.astype(F32)).astype(BF16)
+                return carry
+
+            lax.fori_loop(0, own * kb, split_block, 0)
 
         for n in range(8):
             ox, oy = OFFSETS[n]
@@ -273,29 +294,34 @@
                 ext[own + n, j * SHELL:(j + 1) * SHELL, :] = (marked + roll(value - high, -SHELL, 1)).astype(BF16)
                 ext[own + n, BLK + j * SHELL:BLK + (j + 1) * SHELL, :] = marked.astype(BF16)
 
-        def update(r, carry):
-            span = pl.ds(pl.multiple_of(r * BLK, BLK), BLK)
+        def update(c, carry):
+            span = pl.ds(pl.multiple_of(c * 2 * BLK, 2 * BLK), 2 * BLK)
             temp = prof[0, span, :]
             conc = prof[1, span, :]
             mixed = []
-            for c, value in enumerate((temp, conc)):
+            for d, value in enumerate((temp, conc)):
                 high = value.astype(BF16)
                 low = (value - high.astype(F32)).astype(BF16)
-                both = dot(jnp.concatenate([high, low], axis=1), mixer[c])
+                both = dot(jnp.concatenate([high, low], axis=1), mixer[d])
                 mixed.append(both[:, :BLK] + both[:, BLK:])
-            total = jnp.zeros((BLK, BLK), F32)
-            for k in range(kb):
-                total = total + dot(blocks[r * kb + k], ext[cols_ref[r, k]])
+            totals = []
+            for u in range(2):
+                r = c * 2 + u
+                total = dot(blocks[r * kb], ext[cols_ref[0, r]])
+                for k in range(1, kb):
+                    total = total + dot(blocks[r * kb + k], ext[cols_ref[k, r]])
+                totals.append(total)
+            total = jnp.concatenate(totals, axis=0)
             contact = total + roll(total, SHELL, 1) - roll(total, 2 * SHELL, 1) * temp
             rate = rate_c[span, :] * conc * jnp.exp(0.5 * jnp.tanh(temp - 1.0))
-            new_temp = mixed[0] + rate + jnp.where(in_shell, contact, 0.0)
-            new_temp = new_temp + jnp.where(lane == BLK - 1, cell_ex[span, :], 0.0)
-            live = sub + r * BLK < live_count
+            new_temp = mixed[0] + rate + jnp.where(wide_lane >= BLK - SHELL, contact, 0.0)
+            new_temp = new_temp + jnp.where(wide_lane == BLK - 1, cell_ex[span, :], 0.0)
+            live = wide_sub + c * 2 * BLK < live_count
             prof[0, span, :] = jnp.where(live, new_temp, temp)
             prof[1, span, :] = jnp.where(live, mixed[1] - rate, conc)
             return carry
 
-        lax.fori_loop(0, own, update, 0)
+        lax.fori_loop(0, own // 2, update, 0)
 
         for n in range(4):
             ox, oy = SIDES[n]
@@ -304,22 +330,23 @@
             def _():
                 halo_copy(step, n).wait_recv()
 
-        pop[nxt, 1, 1] = recv_h[step, 0]
-        pop[nxt, 2, cx] = recv_h[step, 1]
-
-        def edges(x, carry):
-            pop[nxt, 3, x + 1, pl.ds(0, 1), :] = recv_h[step, 2, pl.ds(x, 1), :]
-            pop[nxt, 4, x + 1, pl.ds(cy - 1, 1), :] = recv_h[step, 3, pl.ds(x, 1), :]
-            return carry
-
-        lax.fori_loop(0, cx, edges, 0)
-        return carry
-
-    lax.fori_loop(0, STEPS, one_step, 0)
-    store_prof = pltpu.make_async_copy(prof, prof_out, out_sems.at[0])
-    store_pop = pltpu.make_async_copy(pop.at[STEPS % 2, :, pl.ds(1, cx)], pop_out, out_sems.at[1])
-    store_prof.start()
-    store_pop.start()
+        new[1, 1] = recv_h[step, 0]
+        new[2, cx] = recv_h[step, 1]
+
+        def edges(c, carry):
+            for u in range(8):
+                x = c * 8 + u
+                new[3, x + 1, pl.ds(0, 1), :] = recv_h[step, 2, pl.ds(x, 1), :]
+                new[4, x + 1, pl.ds(cy - 1, 1), :] = recv_h[step, 3, pl.ds(x, 1), :]
+            return carry
+
+        lax.fori_loop(0, cx // 8, edges, 0)
+
+    for step in range(STEPS):
+        if step % 2 == 0:
+            one_step(step, pop_a, pop_b)
+        else:
+            one_step(step, pop_b, pop_a)
     for step in range(STEPS):
         for n in range(8):
             @pl.when(there(*OFFSETS[n]))
@@ -329,8 +356,16 @@
             @pl.when(there(*SIDES[n]))
             def _():
                 halo_copy(step, n).wait_send()
+
+
+def store(prof, pop, prof_out, pop_out, sems):
+    cx = pop_out.shape[1]
+    store_pop = pltpu.make_async_copy(pop.at[:, pl.ds(1, cx)], pop_out, sems.at[0])
+    store_prof = pltpu.make_async_copy(prof, prof_out, sems.at[1])
+    store_pop.start()
+    store_prof.start()
+    store_pop.wait()
     store_prof.wait()
-    store_pop.wait()
 
 
 def on_device(
@@ -345,17 +380,22 @@
     vmem = pl.BlockSpec(memory_space=pltpu.VMEM)
     smem = pl.BlockSpec(memory_space=pltpu.SMEM)
     anywhere = pl.BlockSpec(memory_space=pl.ANY)
-    return pl.pallas_call(
+    hbm = pl.BlockSpec(memory_space=pltpu.HBM)
+    state = pl.pallas_call(
         kernel,
         out_shape=(
             jax.ShapeDtypeStruct(profiles.shape, F32),
-            jax.ShapeDtypeStruct(populations.shape, F32),
+            jax.ShapeDtypeStruct((7, cx + 2, cy, nz), F32),
         ),
-        in_specs=[smem, smem, vmem, vmem, vmem, vmem, vmem, anywhere, anywhere, anywhere],
-        out_specs=(anywhere, anywhere),
+        in_specs=[smem, smem] + [hbm] * 8,
+        out_specs=(vmem, vmem),
         scratch_shapes=[
-            pltpu.VMEM(profiles.shape, F32),
-            pltpu.VMEM((2, 7, cx + 2, cy, nz), F32),
+            pltpu.VMEM((7, cx + 2, cy, nz), F32),
+            pltpu.VMEM((own, BLK), F32),
+            pltpu.VMEM((own, BLK), F32),
+            pltpu.VMEM((own, BLK), jnp.int32),
+            pltpu.VMEM((8, BLK), jnp.int32),
+            pltpu.VMEM((2, BLK, BLK), F32),
             pltpu.VMEM((own * kb, BLK, BLK), F32),
             pltpu.VMEM((own * kb, BLK, 2 * BLK), BF16),
             pltpu.VMEM((2, 2 * BLK, 2 * BLK), BF16),
@@ -376,28 +416,43 @@
             pltpu.VMEM((STEPS, 8, SHELL, BLK), F32),
             pltpu.VMEM((STEPS, 4, cx, nz), F32),
             pltpu.VMEM((STEPS, 4, cx, nz), F32),
-            pltpu.SemaphoreType.DMA((3,)),
-            pltpu.SemaphoreType.DMA((2,)),
+            pltpu.SemaphoreType.DMA((8,)),
             pltpu.SemaphoreType.DMA((STEPS, 8)),
             pltpu.SemaphoreType.DMA((STEPS, 8)),
             pltpu.SemaphoreType.DMA((STEPS, 4)),
             pltpu.SemaphoreType.DMA((STEPS, 4)),
         ],
         compiler_params=pltpu.CompilerParams(
-            collective_id=0, has_side_effects=True, vmem_limit_bytes=48 * 1024 * 1024
+            collective_id=0, has_side_effects=True, vmem_limit_bytes=36 * 1024 * 1024
         ),
     )(
         live_count,
-        contact_cols,
-        rate_const.reshape(own, BLK),
-        transfer_coef.reshape(own, BLK),
-        cell_index.reshape(own, BLK),
-        send_lists,
-        radial,
-        profiles,
-        contact_blocks.reshape(own * kb, BLK, BLK),
-        populations,
+        pltpu.with_memory_space_constraint(contact_cols.T, pltpu.HBM),
+        *[
+            pltpu.with_memory_space_constraint(operand, pltpu.HBM)
+            for operand in (
+                rate_const.reshape(own, BLK),
+                transfer_coef.reshape(own, BLK),
+                cell_index.reshape(own, BLK),
+                send_lists,
+                radial,
+                profiles,
+                contact_blocks.reshape(own * kb, BLK, BLK),
+                populations,
+            )
+        ],
     )
+    return pl.pallas_call(
+        store,
+        out_shape=(
+            jax.ShapeDtypeStruct(profiles.shape, F32),
+            jax.ShapeDtypeStruct(populations.shape, F32),
+        ),
+        in_specs=[anywhere, anywhere],
+        out_specs=(hbm, hbm),
+        scratch_shapes=[pltpu.SemaphoreType.DMA((2,))],
+        compiler_params=pltpu.CompilerParams(vmem_limit_bytes=1024 * 1024),
+    )(*state)
 
 
 def solution(mesh):

time: 68.5 us -> 39.8 us (0.58)
  Pallas kernels: 54.2 us -> 38.2 us
  local copies, waits for them, and re-layouts: 12.6 us -> 0 us
    pallas_call x1, Pallas kernels: 54.2 us -> 36 us  [on_device(): pl.pallas_call(kernel, out_shape=(jax.ShapeDtypeStruct(profiles.shape, F3...]
    unnamed x17 -> x0, local copies, waits for them, and re-layouts: 12.6 us -> none
    pallas_call x0 -> x1, Pallas kernels: none -> 2.2 us  [on_device(): pl.pallas_call(store, out_shape=(jax.ShapeDtypeStruct(profiles.shape, F32...]
where the time goes in v1:
time: 39.8 us; the launch traced here: 39.5 us
  Pallas kernels  38.2 us (96%)
  between operations  1.29 us (3%)
    pallas_call x1, Pallas kernels, on_device(): pl.pallas_call(kernel, out_shape=(jax.ShapeDtypeStruct(profiles.shape, F3...  36 us
    pallas_call x1, Pallas kernels, on_device(): pl.pallas_call(store, out_shape=(jax.ShapeDtypeStruct(profiles.shape, F32...  2.2 us

profile of v1, /device:TPU:1, one launch (start us, length us, event | category | flops | bytes accessed | tf_op | source)
XLA Modules:
  0.0 39.5 jit_solution(3698015623667097708)
XLA Ops:
  1.3 36.0 %shard_map.113 = (f32[2,1024,128]{2,1,0:T(8,128)S(1)}, f32[7,34,32,128]{3,2,1,0:T(8,128)S(1)}) custom-call(s32[1]{0:T(128)S(6)} %copy.12.live_ref, s32[4,8]{1,0:T(4,128)} %bitcast.9, f32[8,128]{1,0:T(8,128)} %bitcast.6, f32[8,128]{1,0:T(8,128)} %bitcast.7, s32[8,128]{1,0:T(8,128)} %bitcast.8, s32[8,128]{1,0:T(8,128)} %lists_in.1, f32[2,128,128]{2,1,0:T(8,128)} %radial_in.1, ...), custom_call_target="tpu_custom_call" | custom-call | tf_op jit(solution)/shard_map/pallas_call | solution.py:384
  37.3 2.2 %shard_map.114 = (f32[2,1024,128]{2,1,0:T(8,128)}, f32[7,32,32,128]{3,2,1,0:T(8,128)}) custom-call(f32[2,1024,128]{2,1,0:T(8,128)S(1)} %get-tuple-element.4.prof, f32[7,34,32,128]{3,2,1,0:T(8,128)S(1)} %get-tuple-element.5.pop), custom_call_target="tpu_custom_call" | custom-call | tf_op jit(solution)/shard_map/pallas_call | solution.py:445

commit v2 on v1

--- a/solution.py
+++ b/solution.py
@@ -35,7 +35,7 @@
     prof, pop_b,
     pop_a, rate_ref, coef_ref, cell_ref, lists_ref, radial_ref,
     raw, blocks, mixer, pick, pick_t, listed, zmask, coef, rate_c,
-    shells, ext, theta, theta_s, cell_ex, ex_s, q_ref,
+    shells, ext, theta, theta_s, cell_ex, ex_s,
     send_g, recv_g, send_h, recv_h,
     in_sems, gs_sems, gr_sems, hs_sems, hr_sems,
 ):
@@ -165,9 +165,22 @@
 
         lax.fori_loop(0, own, prepare, 0)
 
-        def gather_ghosts(n, carry):
+        if step == 0:
+            load_pop.wait()
+
+        def ghosts_and_theta(n, carry):
             span = pl.ds(pl.multiple_of(n * 4 * BLK, 4 * BLK), 4 * BLK)
             several = dot(listed[span, :], shells[...])
+            for u in range(cx // 2):
+                x = n * (cx // 2) + u
+                total = old[0, x + 1]
+                for i in range(1, 7):
+                    total = total + old[i, x + 1]
+                theta[x] = total
+                at = pl.ds(pl.multiple_of(x * cy, cy), cy)
+                high = total.astype(BF16)
+                theta_s[at, :nz] = high
+                theta_s[at, nz:] = (total - high.astype(F32)).astype(BF16)
             for m in range(4):
                 found = several[m * BLK:(m + 1) * BLK, :]
                 found = found + roll(found, SHELL, 1) + roll(found, 2 * SHELL, 1)
@@ -178,29 +191,12 @@
                 send_g[step, n * 4 + m] = packed
             return carry
 
-        lax.fori_loop(0, 2, gather_ghosts, 0)
+        lax.fori_loop(0, 2, ghosts_and_theta, 0)
         for n in range(8):
             @pl.when(there(*OFFSETS[n]))
             def _():
                 ghost_copy(step, n).start()
 
-        if step == 0:
-            load_pop.wait()
-
-        def sum_theta(c, carry):
-            for u in range(4):
-                x = c * 4 + u
-                total = old[0, x + 1]
-                for i in range(1, 7):
-                    total = total + old[i, x + 1]
-                theta[x] = total
-                span = pl.ds(pl.multiple_of(x * cy, cy), cy)
-                high = total.astype(BF16)
-                theta_s[span, :nz] = high
-                theta_s[span, nz:] = (total - high.astype(F32)).astype(BF16)
-            return carry
-
-        lax.fori_loop(0, cx // 4, sum_theta, 0)
         ones = jnp.ones((2 * nz, BLK), BF16)
 
         def gather_theta(c, carry):
@@ -219,40 +215,36 @@
             return carry
 
         lax.fori_loop(0, own // 4, gather_theta, 0)
-        slabs = 4 * BLK // cy
-
-        def scatter(c, carry):
-            span = pl.ds(pl.multiple_of(c * 4 * BLK, 4 * BLK), 4 * BLK)
-            found = dot(pick_t[span, :], ex_s[...])
-            some = pl.ds(c * slabs, slabs)
-            total = (found[:, :nz] + found[:, nz:]).reshape(slabs, cy, nz)
-            q_ref[some] = 1.25 * theta[some] - 0.5 * total
+        slabs = 2 * BLK // cy
+        zlane = lax.broadcasted_iota(jnp.int32, (cy, nz), 1)
+
+        def scatter_and_stream(c, carry):
+            founds = []
+            for v in range(2):
+                start = pl.multiple_of((c * 2 + v) * 2 * BLK, 2 * BLK)
+                founds.append(dot(pick_t[pl.ds(start, 2 * BLK), :], ex_s[...]))
+            for v in range(2):
+                source = founds[v][:, :nz] + founds[v][:, nz:]
+                for u in range(slabs):
+                    x = (c * 2 + v) * slabs + u
+                    q = 1.25 * theta[x] - 0.5 * source[u * cy:(u + 1) * cy, :]
+                    part = 0.125 * q
+                    new[0, x + 1] = 0.25 * (q - old[0, x + 1])
+                    new[1, x + 2] = part - 0.25 * old[1, x + 1]
+                    new[2, x] = part - 0.25 * old[2, x + 1]
+                    up = roll(part - 0.25 * old[3, x + 1], 1, 0)
+                    down = roll(part - 0.25 * old[4, x + 1], -1, 0)
+                    new[3, x + 1] = up
+                    new[4, x + 1] = down
+                    send_h[step, 2, pl.ds(x, 1), :] = up[:1]
+                    send_h[step, 3, pl.ds(x, 1), :] = down[cy - 1:]
+                    above = roll(part - 0.25 * old[5, x + 1], 1, 1)
+                    below = roll(part - 0.25 * old[6, x + 1], -1, 1)
+                    new[5, x + 1] = jnp.where(zlane == 0, 0.0, above)
+                    new[6, x + 1] = jnp.where(zlane == nz - 1, 0.0, below)
             return carry
 
-        lax.fori_loop(0, rows // (4 * BLK), scatter, 0)
-        zlane = lax.broadcasted_iota(jnp.int32, (cy, nz), 1)
-
-        def stream(c, carry):
-            for u in range(2):
-                x = c * 2 + u
-                q = q_ref[x]
-                part = 0.125 * q
-                new[0, x + 1] = 0.25 * (q - old[0, x + 1])
-                new[1, x + 2] = part - 0.25 * old[1, x + 1]
-                new[2, x] = part - 0.25 * old[2, x + 1]
-                up = roll(part - 0.25 * old[3, x + 1], 1, 0)
-                down = roll(part - 0.25 * old[4, x + 1], -1, 0)
-                new[3, x + 1] = up
-                new[4, x + 1] = down
-                send_h[step, 2, pl.ds(x, 1), :] = up[:1]
-                send_h[step, 3, pl.ds(x, 1), :] = down[cy - 1:]
-                above = roll(part - 0.25 * old[5, x + 1], 1, 1)
-                below = roll(part - 0.25 * old[6, x + 1], -1, 1)
-                new[5, x + 1] = jnp.where(zlane == 0, 0.0, above)
-                new[6, x + 1] = jnp.where(zlane == nz - 1, 0.0, below)
-            return carry
-
-        lax.fori_loop(0, cx // 2, stream, 0)
+        lax.fori_loop(0, rows // (4 * BLK), scatter_and_stream, 0)
         send_h[step, 0] = new[1, cx + 1]
         send_h[step, 1] = new[2, 0]
         for n in range(4):
@@ -263,14 +255,15 @@
         if step == 0:
             load_blocks.wait()
 
-            def split_block(i, carry):
-                value = raw[i]
-                high = value.astype(BF16)
-                blocks[i, :, :BLK] = high
-                blocks[i, :, BLK:] = (value - high.astype(F32)).astype(BF16)
+            def split_blocks(r, carry):
+                for k in range(kb):
+                    value = raw[r * kb + k]
+                    high = value.astype(BF16)
+                    blocks[r * kb + k, :, :BLK] = high
+                    blocks[r * kb + k, :, BLK:] = (value - high.astype(F32)).astype(BF16)
                 return carry
 
-            lax.fori_loop(0, own * kb, split_block, 0)
+            lax.fori_loop(0, own, split_blocks, 0)
 
         for n in range(8):
             ox, oy = OFFSETS[n]
@@ -294,8 +287,8 @@
                 ext[own + n, j * SHELL:(j + 1) * SHELL, :] = (marked + roll(value - high, -SHELL, 1)).astype(BF16)
                 ext[own + n, BLK + j * SHELL:BLK + (j + 1) * SHELL, :] = marked.astype(BF16)
 
-        def update(c, carry):
-            span = pl.ds(pl.multiple_of(c * 2 * BLK, 2 * BLK), 2 * BLK)
+        def update(c):
+            span = pl.ds(c * 2 * BLK, 2 * BLK)
             temp = prof[0, span, :]
             conc = prof[1, span, :]
             mixed = []
@@ -319,9 +312,9 @@
             live = wide_sub + c * 2 * BLK < live_count
             prof[0, span, :] = jnp.where(live, new_temp, temp)
             prof[1, span, :] = jnp.where(live, mixed[1] - rate, conc)
-            return carry
-
-        lax.fori_loop(0, own // 2, update, 0)
+
+        for c in range(own // 2):
+            update(c)
 
         for n in range(4):
             ox, oy = SIDES[n]
@@ -411,7 +404,6 @@
             pltpu.VMEM((rows, 2 * nz), BF16),
             pltpu.VMEM((slots, BLK), F32),
             pltpu.VMEM((slots, 2 * nz), BF16),
-            pltpu.VMEM((cx, cy, nz), F32),
             pltpu.VMEM((STEPS, 8, SHELL, BLK), F32),
             pltpu.VMEM((STEPS, 8, SHELL, BLK), F32),
             pltpu.VMEM((STEPS, 4, cx, nz), F32),

time: 39.8 us -> 34.9 us (0.88)
  Pallas kernels: 38.2 us -> 33 us
    pallas_call x1, Pallas kernels: 36 us -> 30.8 us  [on_device(): pl.pallas_call(kernel, out_shape=(jax.ShapeDtypeStruct(profiles.shape, F3...]
where the time goes in v2:
time: 34.9 us; the launch traced here: 34.3 us
  Pallas kernels  33 us (95%)
  between operations  1.29 us (4%)
    pallas_call x1, Pallas kernels, on_device(): pl.pallas_call(kernel, out_shape=(jax.ShapeDtypeStruct(profiles.shape, F3...  30.8 us
    pallas_call x1, Pallas kernels, on_device(): pl.pallas_call(store, out_shape=(jax.ShapeDtypeStruct(profiles.shape, F32...  2.2 us

profile of v2, /device:TPU:1, one launch (start us, length us, event | category | flops | bytes accessed | tf_op | source)
XLA Modules:
  0.0 34.3 jit_solution(12879180239198886018)
XLA Ops:
  1.3 30.8 %shard_map.113 = (f32[2,1024,128]{2,1,0:T(8,128)S(1)}, f32[7,34,32,128]{3,2,1,0:T(8,128)S(1)}) custom-call(s32[1]{0:T(128)S(6)} %copy.12.live_ref, s32[4,8]{1,0:T(4,128)} %bitcast.9, f32[8,128]{1,0:T(8,128)} %bitcast.6, f32[8,128]{1,0:T(8,128)} %bitcast.7, s32[8,128]{1,0:T(8,128)} %bitcast.8, s32[8,128]{1,0:T(8,128)} %lists_in.1, f32[2,128,128]{2,1,0:T(8,128)} %radial_in.1, ...), custom_call_target="tpu_custom_call" | custom-call | tf_op jit(solution)/shard_map/pallas_call | solution.py:377
  32.1 2.2 %shard_map.114 = (f32[2,1024,128]{2,1,0:T(8,128)}, f32[7,32,32,128]{3,2,1,0:T(8,128)}) custom-call(f32[2,1024,128]{2,1,0:T(8,128)S(1)} %get-tuple-element.4.prof, f32[7,34,32,128]{3,2,1,0:T(8,128)S(1)} %get-tuple-element.5.pop), custom_call_target="tpu_custom_call" | custom-call | tf_op jit(solution)/shard_map/pallas_call | solution.py:437

commit v3 on v2

--- a/solution.py
+++ b/solution.py
@@ -35,7 +35,7 @@
     prof, pop_b,
     pop_a, rate_ref, coef_ref, cell_ref, lists_ref, radial_ref,
     raw, blocks, mixer, pick, pick_t, listed, zmask, coef, rate_c,
-    shells, ext, theta, theta_s, cell_ex, ex_s,
+    shells, ext, theta, theta_s, cell_ex, ex_s, fresh,
     send_g, recv_g, send_h, recv_h,
     in_sems, gs_sems, gr_sems, hs_sems, hr_sems,
 ):
@@ -205,7 +205,19 @@
             mask = zmask[span, :]
             kept = jnp.concatenate([found[:, :nz] * mask, found[:, nz:] * mask], axis=1).astype(BF16)
             at_cell = dot(kept, ones)
-            last = jnp.broadcast_to(prof[0, span, BLK - 1:], (4 * BLK, BLK))
+            temp = prof[0, span, :]
+            conc = prof[1, span, :]
+            mixed = []
+            for d, part in enumerate((temp, conc)):
+                high = part.astype(BF16)
+                low = (part - high.astype(F32)).astype(BF16)
+                both = dot(jnp.concatenate([high, low], axis=1), mixer[d])
+                mixed.append(both[:, :BLK] + both[:, BLK:])
+            rate = rate_c[span, :] * conc * jnp.exp(0.5 * jnp.tanh(temp - 1.0))
+            fresh[span, :] = mixed[0] + rate
+            live = lax.broadcasted_iota(jnp.int32, (4 * BLK, BLK), 0) + c * 4 * BLK < live_count
+            prof[1, span, :] = jnp.where(live, mixed[1] - rate, conc)
+            last = jnp.broadcast_to(temp[:, BLK - 1:], (4 * BLK, BLK))
             value = coef[span, :] * (at_cell - last)
             cell_ex[span, :] = value
             value = value * mask
@@ -290,13 +302,6 @@
         def update(c):
             span = pl.ds(c * 2 * BLK, 2 * BLK)
             temp = prof[0, span, :]
-            conc = prof[1, span, :]
-            mixed = []
-            for d, value in enumerate((temp, conc)):
-                high = value.astype(BF16)
-                low = (value - high.astype(F32)).astype(BF16)
-                both = dot(jnp.concatenate([high, low], axis=1), mixer[d])
-                mixed.append(both[:, :BLK] + both[:, BLK:])
             totals = []
             for u in range(2):
                 r = c * 2 + u
@@ -306,12 +311,10 @@
                 totals.append(total)
             total = jnp.concatenate(totals, axis=0)
             contact = total + roll(total, SHELL, 1) - roll(total, 2 * SHELL, 1) * temp
-            rate = rate_c[span, :] * conc * jnp.exp(0.5 * jnp.tanh(temp - 1.0))
-            new_temp = mixed[0] + rate + jnp.where(wide_lane >= BLK - SHELL, contact, 0.0)
+            new_temp = fresh[span, :] + jnp.where(wide_lane >= BLK - SHELL, contact, 0.0)
             new_temp = new_temp + jnp.where(wide_lane == BLK - 1, cell_ex[span, :], 0.0)
             live = wide_sub + c * 2 * BLK < live_count
             prof[0, span, :] = jnp.where(live, new_temp, temp)
-            prof[1, span, :] = jnp.where(live, mixed[1] - rate, conc)
 
         for c in range(own // 2):
             update(c)
@@ -404,6 +407,7 @@
             pltpu.VMEM((rows, 2 * nz), BF16),
             pltpu.VMEM((slots, BLK), F32),
             pltpu.VMEM((slots, 2 * nz), BF16),
+            pltpu.VMEM((slots, BLK), F32),
             pltpu.VMEM((STEPS, 8, SHELL, BLK), F32),
             pltpu.VMEM((STEPS, 8, SHELL, BLK), F32),
             pltpu.VMEM((STEPS, 4, cx, nz), F32),

time: 34.9 us -> 37.2 us (1.066)
  Pallas kernels: 33 us -> 35.3 us
    pallas_call x1, Pallas kernels: 30.8 us -> 33.1 us  [on_device(): pl.pallas_call(kernel, out_shape=(jax.ShapeDtypeStruct(profiles.shape, F3...]
where the time goes in v3:
time: 37.2 us; the launch traced here: 36.6 us
  Pallas kernels  35.3 us (95%)
  between operations  1.29 us (3%)
    pallas_call x1, Pallas kernels, on_device(): pl.pallas_call(kernel, out_shape=(jax.ShapeDtypeStruct(profiles.shape, F3...  33.1 us
    pallas_call x1, Pallas kernels, on_device(): pl.pallas_call(store, out_shape=(jax.ShapeDtypeStruct(profiles.shape, F32...  2.2 us

profile of v3, /device:TPU:1, one launch (start us, length us, event | category | flops | bytes accessed | tf_op | source)
XLA Modules:
  0.0 36.6 jit_solution(8191938832517714552)
XLA Ops:
  1.3 33.1 %shard_map.113 = (f32[2,1024,128]{2,1,0:T(8,128)S(1)}, f32[7,34,32,128]{3,2,1,0:T(8,128)S(1)}) custom-call(s32[1]{0:T(128)S(6)} %copy.12.live_ref, s32[4,8]{1,0:T(4,128)} %bitcast.9, f32[8,128]{1,0:T(8,128)} %bitcast.6, f32[8,128]{1,0:T(8,128)} %bitcast.7, s32[8,128]{1,0:T(8,128)} %bitcast.8, s32[8,128]{1,0:T(8,128)} %lists_in.1, f32[2,128,128]{2,1,0:T(8,128)} %radial_in.1, ...), custom_call_target="tpu_custom_call" | custom-call | tf_op jit(solution)/shard_map/pallas_call | solution.py:380
  34.4 2.2 %shard_map.114 = (f32[2,1024,128]{2,1,0:T(8,128)}, f32[7,32,32,128]{3,2,1,0:T(8,128)}) custom-call(f32[2,1024,128]{2,1,0:T(8,128)S(1)} %get-tuple-element.4.prof, f32[7,34,32,128]{3,2,1,0:T(8,128)S(1)} %get-tuple-element.5.pop), custom_call_target="tpu_custom_call" | custom-call | tf_op jit(solution)/shard_map/pallas_call | solution.py:441
